TPU v7x, 256 devices: a whole 4x4x8 slice. The times are simulated.
256 devices in a mesh: dp: 16 (over y_lo, z), seq: 16 (over x, y_hi, core).
Axes of the slice: x: 4, y: 4 (y_hi: 2, y_lo: 2; y = y_hi * 2 + y_lo), z: 8, core: 2. Of those that a mesh axis runs over, the one named last changes fastest.
Arguments:
- seq_embed: bfloat16 [16, 3072, 1536], P('dp', 'seq'), may hold values from -24 to 24
- w_qkv: bfloat16 [1536, 2304], P('seq'), may hold values from -1 to 1
- upstream: bfloat16 [16, 3072, 768], P('dp', 'seq'), may hold values from -6 to 6
Outputs:
- attended: bfloat16 [16, 3072, 768], P('dp', 'seq')
- grad_input: bfloat16 [16, 3072, 1536], P('dp', 'seq')
- grad_qkv: bfloat16 [1536, 2304], P('seq')
All inputs are finite; a program needn't handle non-finite values.
Results may differ from a plain program's by a relative error of at most 0.04.
Values may be sent and summed in bfloat16 or wider, within the bound.
A program may use at most 128 MiB of HBM per device.

v0:
```python
import math
import jax
import jax.numpy as jnp
from jax import lax
from jax.sharding import PartitionSpec as P

HEADS = 6


def split_heads(block, heads):
    return block.reshape(block.shape[0], heads, block.shape[1] // heads)


def on_device(seq_embed, w_qkv, upstream):
    heads = HEADS
    width = upstream.shape[-1]
    head_dim = width // heads
    score_scale = 1.0 / math.sqrt(head_dim)
    weights = lax.all_gather(w_qkv, "seq", axis=0, tiled=True)
    tokens = seq_embed[0]
    grad_out = upstream[0]
    rows_here = tokens.shape[0]
    projected = jnp.dot(tokens, weights, preferred_element_type=jnp.float32).astype(jnp.bfloat16)
    queries = projected[:, :width]
    keys_here = projected[:, width : 2 * width]
    values_here = projected[:, 2 * width :]
    keys_all, values_all = (
        lax.all_gather(keys_here, "seq", axis=0, tiled=True),
        lax.all_gather(values_here, "seq", axis=0, tiled=True),
    )
    query_heads = split_heads(queries, heads)
    key_heads = split_heads(keys_all, heads)
    value_heads = split_heads(values_all, heads)
    scores = (
        jnp.einsum("qhd,khd->hqk", query_heads, key_heads, preferred_element_type=jnp.float32)
        * score_scale
    )
    peak = jnp.max(scores, axis=-1, keepdims=True)
    log_total = peak[..., 0] + jnp.log(jnp.sum(jnp.exp(scores - peak), axis=-1))
    probs = jnp.exp(scores - log_total[..., None])
    probs_low = probs.astype(jnp.bfloat16)
    attended_heads = jnp.einsum(
        "hqk,khd->qhd", probs_low, value_heads, preferred_element_type=jnp.float32
    ).astype(jnp.bfloat16)
    grad_heads = split_heads(grad_out, heads)
    delta_rows = jnp.sum(
        grad_heads.astype(jnp.float32) * attended_heads.astype(jnp.float32), axis=-1
    )
    grad_probs = jnp.einsum(
        "qhd,khd->hqk", grad_heads, value_heads, preferred_element_type=jnp.float32
    )
    grad_scores = (probs * (grad_probs - delta_rows.T[..., None]) * score_scale).astype(
        jnp.bfloat16
    )
    grad_queries = jnp.einsum(
        "hqk,khd->qhd", grad_scores, key_heads, preferred_element_type=jnp.float32
    ).astype(jnp.bfloat16)
    lse_all, delta_all = (
        lax.all_gather(log_total.T, "seq", axis=0, tiled=True),
        lax.all_gather(delta_rows, "seq", axis=0, tiled=True),
    )
    key_local = split_heads(keys_here, heads)
    value_local = split_heads(values_here, heads)
    query_piece = split_heads(lax.all_gather(queries, "seq", axis=0, tiled=True), heads)
    grad_piece = split_heads(lax.all_gather(grad_out, "seq", axis=0, tiled=True), heads)
    lse_piece = lse_all.T
    delta_piece = delta_all.T
    piece_scores = (
        jnp.einsum("qhd,khd->hqk", query_piece, key_local, preferred_element_type=jnp.float32)
        * score_scale
    )
    piece_probs = jnp.exp(piece_scores - lse_piece[..., None])
    grad_values = jnp.einsum(
        "hqk,qhd->khd",
        piece_probs.astype(jnp.bfloat16),
        grad_piece,
        preferred_element_type=jnp.float32,
    )
    piece_grad_probs = jnp.einsum(
        "qhd,khd->hqk", grad_piece, value_local, preferred_element_type=jnp.float32
    )
    piece_grad_scores = (
        piece_probs * (piece_grad_probs - delta_piece[..., None]) * score_scale
    ).astype(jnp.bfloat16)
    grad_keys = jnp.einsum(
        "hqk,qhd->khd", piece_grad_scores, query_piece, preferred_element_type=jnp.float32
    )
    grad_keys, grad_values = (grad_keys, grad_values)
    grad_proj = jnp.concatenate(
        [
            grad_queries.reshape(rows_here, width),
            grad_keys.astype(jnp.bfloat16).reshape(rows_here, width),
            grad_values.astype(jnp.bfloat16).reshape(rows_here, width),
        ],
        axis=1,
    )
    grad_input = lax.dot_general(
        grad_proj, weights, (((1,), (1,)), ((), ())), preferred_element_type=jnp.float32
    ).astype(jnp.bfloat16)
    term = lax.dot_general(
        tokens, grad_proj, (((0,), (0,)), ((), ())), preferred_element_type=jnp.float32
    )
    summed = lax.psum_scatter(
        lax.optimization_barrier(term.astype(jnp.bfloat16))
        .astype(jnp.float32)
        .astype(jnp.bfloat16),
        "seq",
        scatter_dimension=0,
        tiled=True,
    )
    total = lax.psum(summed, "dp").astype(jnp.float32)
    attended = attended_heads.reshape(rows_here, width)
    return (attended[None], grad_input[None], total.astype(jnp.bfloat16))


def solution(mesh):
    placed = (P("dp", "seq", None), P("seq", None), P("dp", "seq", None))
    return jax.shard_map(
        on_device,
        mesh=mesh,
        in_specs=placed,
        out_specs=(P("dp", "seq", None), P("dp", "seq", None), P("seq", None)),
        check_vma=False,
    )
```

profile of v0, /device:TPU:2, one launch (start us, length us, event | category | flops | bytes accessed | tf_op | source)
XLA Modules:
  0.0 663.6 jit_solution(6117910122317396261)
XLA Ops:
  7.2 0.7 all-gather.9.cloned.1.call-update
  8.0 0.7 all-gather.17.cloned.1.call-update
  8.7 76.5 %all-gather.9.cloned.1.call-done = bf16[1536,2304]{1,0:T(8,128)(2,1)} async-done(((bf16[96,2304]{1,0:T(8,128)(2,1)}), bf16[1536,2304]{1,0:T(8,128)(2,1)}) %all-gather.9.cloned.1.call-update) | async-done | bytes 7077904 | tf_op jit(solution)/shard_map/all_gather | solution.py:19
  85.2 4.5 convolution_convert_fusion.1
  89.7 1.0 slice_bitcast_fusion.2
  90.8 0.5 all-gather.13.cloned.1.call-update
  91.4 0.5 all-gather.15.cloned.1.call-update
  92.3 57.5 %all-gather.17.cloned.1.call-done = bf16[1,3072,768]{2,1,0:T(8,128)(2,1)} async-done(((bf16[1,192,768]{2,1,0:T(8,128)(2,1)}), bf16[1,3072,768]{2,1,0:T(8,128)(2,1)}) %all-gather.17.cloned.1.call-update) | async-done | bytes 4718608 | tf_op jit(solution)/shard_map/all_gather | solution.py:65
  149.8 6.7 %copy.47 = bf16[1,3072,768]{1,2,0:T(8,128)(2,1)} copy(bf16[1,3072,768]{2,1,0:T(8,128)(2,1)} %all-gather.17.cloned.1.call-done) | data formatting | bytes 9437184 | tf_op jit(solution)/shard_map/all_gather | solution.py:65
  156.5 58.5 %all-gather.11.cloned.1.call-done = bf16[3072,768]{1,0:T(8,128)(2,1)} async-done(((bf16[192,768]{1,0:T(8,128)(2,1)}), bf16[3072,768]{1,0:T(8,128)(2,1)}) %all-gather.11.cloned.1.call-update) | async-done | bytes 4718608 | tf_op jit(solution)/shard_map/all_gather | solution.py:29
  215.0 6.7 %copy.32 = bf16[3072,768]{0,1:T(8,128)(2,1)} copy(bf16[3072,768]{1,0:T(8,128)(2,1)} %all-gather.11.cloned.1.call-done) | data formatting | bytes 9437184 | tf_op jit(solution)/shard_map/all_gather | solution.py:29
  221.7 58.3 %all-gather.13.cloned.1.call-done = bf16[3072,768]{1,0:T(8,128)(2,1)} async-done(((bf16[192,768]{1,0:T(8,128)(2,1)}), bf16[3072,768]{1,0:T(8,128)(2,1)}) %all-gather.13.cloned.1.call-update) | async-done | bytes 4718608 | tf_op jit(solution)/shard_map/all_gather | solution.py:28
  280.0 6.7 %copy.33 = bf16[3072,768]{0,1:T(8,128)(2,1)} copy(bf16[3072,768]{1,0:T(8,128)(2,1)} %all-gather.13.cloned.1.call-done) | data formatting | bytes 9437184 | tf_op jit(solution)/shard_map/all_gather | solution.py:28
  286.7 9.6 %multiply_reduce_fusion = (f32[6,192]{1,0:T(8,128)S(1)}, f32[6,192,3072]{2,1,0:T(8,128)}) fusion(bf16[3072,6,128]{0,2,1:T(8,128)(2,1)} %bitcast.94, bf16[24,6,8,128]{3,2,1,0:T(8,128)(2,1)S(1)} %get-tuple-element.13), kind=kOutput, calls=%fused_computation.11 | convolution fusion | flops 913046400 | bytes 19173888 | tf_op jit(solution)/shard_map/qhd,khd->hqk/dot_general | solution.py:35
  296.3 7.5 %exponential_reduce_fusion = f32[6,192]{1,0:T(8,128)S(1)} fusion(f32[6,192,3072]{2,1,0:T(8,128)} %get-tuple-element.19, f32[6,192]{1,0:T(8,128)S(1)} %get-tuple-element.18), kind=kLoop, calls=%fused_computation.8 | loop fusion | flops 10615680 | bytes 14164992 | tf_op jit(solution)/shard_map/reduce_sum | solution.py:39
  303.8 8.5 %multiply_reduce_fusion.1 = (f32[192,6]{0,1:T(8,128)S(1)}, bf16[192,6,128]{2,0,1:T(8,128)(2,1)}) fusion(bf16[192,6,128]{2,1,0:T(8,128)(2,1)S(1)} %reshape_squeeze.3, bf16[3072,6,128]{0,2,1:T(8,128)(2,1)S(1)} %bitcast.103, f32[6,192,3072]{2,1,0:T(8,128)} %get-tuple-element.19, f32[6,192]{1,0:T(8,128)S(1)} %log_add_fusion), kind=kOutput, calls=%fused_computation.37 | convolution fusion | flops 917322624 | bytes 19473408 | tf_op jit(solution)/shard_map/hqk,khd->qhd/dot_general | solution.py:42
  312.3 20.3 %all-gather.2 = f32[16,192,6]{1,2,0:T(8,128)S(1)} all-gather(f32[1,192,6]{1,2,0:T(8,128)S(1)} %bitcast.108), channel_id=1, replica_groups=mesh['dp'=16,'seq'=16] {'seq'}, dimensions={0}, use_global_device_ids=true | all-gather | bytes 78336 | tf_op jit(solution)/shard_map/all_gather | solution.py:60
  332.8 20.5 %all-gather.1 = f32[16,192,6]{1,2,0:T(8,128)S(1)} all-gather(f32[1,192,6]{1,2,0:T(8,128)S(1)} %bitcast.107), channel_id=1, replica_groups=mesh['dp'=16,'seq'=16] {'seq'}, dimensions={0}, use_global_device_ids=true | all-gather | bytes 78336 | tf_op jit(solution)/shard_map/all_gather | solution.py:59
  353.5 10.7 %fusion.42 = bf16[6,24,8,128]{3,2,1,0:T(8,128)(2,1)S(1)} fusion(bf16[3072,6,128]{0,2,1:T(8,128)(2,1)} %bitcast.95, f32[6,192,3072]{2,1,0:T(8,128)} %get-tuple-element.19, f32[6,192]{1,0:T(8,128)S(1)} %bitcast.109, f32[6,192]{1,0:T(8,128)S(1)} %log_add_fusion, bf16[3072,6,128]{0,2,1:T(8,128)(2,1)} %bitcast.100, bf16[192,6,128]{2,1,0:T(8,128)(2,1)S(1)} %reshape_squeeze.3), kind=kOutput, calls=%fused_computation.33 | convolution fusion | flops 1833320448 | bytes 24192000 | tf_op jit(solution)/shard_map/hqk,khd->qhd/dot_general | solution.py:55
  364.3 6.7 %copy.43 = bf16[3072,768]{0,1:T(8,128)(2,1)} copy(bf16[3072,768]{1,0:T(8,128)(2,1)} %all-gather.15.cloned.1.call-done) | data formatting | bytes 9437184 | tf_op jit(solution)/shard_map/all_gather | solution.py:64
  371.0 9.4 %fusion.54 = f32[6,3072,192]{1,2,0:T(8,128)} fusion(bf16[3072,6,128]{0,2,1:T(8,128)(2,1)} %bitcast.96, bf16[24,6,8,128]{3,2,1,0:T(8,128)(2,1)S(1)} %get-tuple-element.14), kind=kOutput, calls=%fused_computation.43 | convolution fusion | flops 905969664 | bytes 19169280 | tf_op jit(solution)/shard_map/qhd,khd->hqk/dot_general | solution.py:69
  380.3 8.8 %fusion.36 = bf16[6,24,8,128]{3,2,1,0:T(8,128)(2,1)S(1)} fusion(bf16[3072,6,128]{0,2,1:T(8,128)(2,1)} %bitcast.98, f32[6,3072,192]{1,2,0:T(8,128)} %fusion.54, f32[6,3072]{1,0:T(8,128)S(1)} %bitcast.105), kind=kOutput, calls=%fused_computation.31 | convolution fusion | flops 916733952 | bytes 19243008 | tf_op jit(solution)/shard_map/hqk,qhd->khd/dot_general | solution.py:73
  389.1 10.9 %fusion.45 = bf16[6,24,8,128]{3,2,1,0:T(8,128)(2,1)S(1)} fusion(bf16[3072,6,128]{0,2,1:T(8,128)(2,1)} %bitcast.97, f32[6,3072,192]{1,2,0:T(8,128)} %fusion.54, f32[6,3072]{1,0:T(8,128)S(1)} %bitcast.104, f32[6,3072]{1,0:T(8,128)} %bitcast.106, bf16[3072,6,128]{0,2,1:T(8,128)(2,1)} %bitcast.99, bf16[24,6,8,128]{3,2,1,0:T(8,128)(2,1)S(1)} %get-tuple-element.12), kind=kOutput, calls=%fused_computation.34 | convolution fusion | flops 1833320448 | bytes 24330240 | tf_op jit(solution)/shard_map/hqk,qhd->khd/dot_general | solution.py:85
  400.1 5.0 fusion.6
  405.1 9.8 %copy.64 = bf16[1536,2304]{1,0:T(8,128)(2,1)} copy(bf16[1536,2304]{0,1:T(8,128)(2,1)} %fusion.6) | data formatting | bytes 14155776
  415.0 0.9 copy-done.2
  416.1 1.1 broadcast_in_dim_reshape.3
  417.1 99.5 %reduce-scatter.4.cloned.1.call-done = bf16[96,2304]{1,0:T(8,128)(2,1)} async-done(((bf16[1536,2304]{1,0:T(8,128)(2,1)}), bf16[96,2304]{1,0:T(8,128)(2,1)}) %reduce-scatter.4.cloned.1.call-update) | async-done | bytes 442384
  516.7 2.1 copy.65
  518.8 6.3 fusion.23
  525.0 129.7 %all-reduce.2.cloned.1.call-done = bf16[96,2304]{0,1:T(8,128)(2,1)} async-done(((bf16[96,2304]{0,1:T(8,128)(2,1)}), bf16[96,2304]{0,1:T(8,128)(2,1)}) %all-reduce.2.cloned.1.call-update) | async-done | bytes 442384 | tf_op jit(solution)/shard_map/psum | solution.py:111
  654.7 2.1 copy.55
  (33 shorter events, 1.3 us)
Async XLA Ops:
  7.2 78.0 %copy-start = (bf16[1,192,1536]{2,1,0:T(8,128)(2,1)S(1)}, bf16[1,192,1536]{2,1,0:T(8,128)(2,1)}, u32[]{:S(2)}) copy-start(bf16[1,192,1536]{2,1,0:T(8,128)(2,1)} %param.3) | copy-start | bytes 1769476
  7.2 78.0 %all-gather.9.cloned.1.call-start = ((), (), s32[]{:S(2)}) async-start(), calls=%async_computation.1 | async-start | bytes 7520256 | tf_op jit(solution)/shard_map/all_gather | solution.py:19
  7.9 141.9 %all-gather.17.cloned.1.call-start = ((), (), s32[]{:S(2)}) async-start(), calls=%async_computation.6 | async-start | bytes 5013504 | tf_op jit(solution)/shard_map/all_gather | solution.py:65
  8.7 83.3 %copy-start.1 = (bf16[1,192,768]{2,1,0:T(8,128)(2,1)S(1)}, bf16[1,192,768]{2,1,0:T(8,128)(2,1)}, u32[]{:S(2)}) copy-start(bf16[1,192,768]{2,1,0:T(8,128)(2,1)} %param.5) | copy-start | bytes 884740
  8.7 206.3 %all-gather.11.cloned.1.call-start = ((), (), s32[]{:S(2)}) async-start(), calls=%async_computation.2 | async-start | bytes 5013504 | tf_op jit(solution)/shard_map/all_gather | solution.py:29
  90.8 189.2 %all-gather.13.cloned.1.call-start = ((), (), s32[]{:S(2)}) async-start(), calls=%async_computation.3 | async-start | bytes 5013504 | tf_op jit(solution)/shard_map/all_gather | solution.py:28
  91.3 272.9 %all-gather.15.cloned.1.call-start = ((), (), s32[]{:S(2)}) async-start(), calls=%async_computation.4 | async-start | bytes 5013504 | tf_op jit(solution)/shard_map/all_gather | solution.py:64
  91.9 424.7 %reduce-scatter.4.cloned.1.call-start = ((), (), s32[]{:S(2)}) async-start(), calls=%async_computation.7 | async-start | bytes 7520256
  280.0 23.8 %slice-start = ((s8[4718592]{0:T(1024)(128)(4,1)}), s8[524288]{0:T(1024)(128)(4,1)S(1)}, s32[]{:S(2)}) async-start(s8[4718592]{0:T(1024)(128)(4,1)} %bitcast.101), calls=%async_computation.8 | async-start | bytes 1048576
  286.7 17.1 %slice-start.1 = ((s8[4718592]{0:T(1024)(128)(4,1)}), s8[4194304]{0:T(1024)(128)(4,1)S(1)}, s32[]{:S(2)}) async-start(s8[4718592]{0:T(1024)(128)(4,1)} %bitcast.101), calls=%async_computation.9 | async-start | bytes 8388608
  353.5 26.9 %copy-start.3 = (f32[3072,6]{0,1:T(8,128)}, f32[3072,6]{0,1:T(8,128)S(1)}, u32[]{:S(2)}) copy-start(f32[3072,6]{0,1:T(8,128)S(1)} %reshape.59) | copy-start | bytes 221188
  414.9 1.0 copy-start.2
  414.9 239.8 %all-reduce.2.cloned.1.call-start = ((), (), s32[]{:S(2)}) async-start(), calls=%async_computation.5 | async-start | bytes 1179648 | tf_op jit(solution)/shard_map/psum | solution.py:111
Sparse Core Ops, SparseCore 0:
  10.7 74.4 all-gather.8
  87.9 61.8 all-gather.16
  153.1 61.8 all-gather.10
  218.1 61.8 all-gather.12
  283.1 62.3 all-gather.14
  415.0 101.5 reduce-scatter.3
  519.3 135.3 all-reduce.1
where the time goes:
time: 665 us; the launch traced here: 664 us
  waiting for transfers between devices  482 us (72%)
  matrix products  73.6 us (11%)
  local copies, waits for them, and re-layouts  44.6 us (7%)
  blocking collectives  40.9 us (6%)
  between operations  14.3 us (2%)
  other arithmetic  7.47 us (1%)
    psum x1, waiting for transfers between devices, on_device(): total = lax.psum(summed, 'dp').astype(jnp.float32)  130 us
    unnamed x8, waiting for transfers between devices  102 us
    all_gather x1, waiting for transfers between devices, on_device(): weights = lax.all_gather(w_qkv, 'seq', axis=0, tiled=True)  76.5 us
    all_gather x1, waiting for transfers between devices, on_device(): lax.all_gather(values_here, 'seq', axis=0, tiled=True)  58.5 us
    all_gather x1, waiting for transfers between devices, on_device(): lax.all_gather(keys_here, 'seq', axis=0, tiled=True)  58.3 us
    all_gather x1, waiting for transfers between devices, on_device(): lax.all_gather(grad_out, 'seq', axis=0, tiled=True)  57.5 us
    all_gather x1, blocking collectives, on_device(): lax.all_gather(log_total.T, 'seq', axis=0, tiled=True)  20.5 us
    all_gather x1, blocking collectives, on_device(): lax.all_gather(delta_rows, 'seq', axis=0, tiled=True)  20.3 us
  transfers between devices with their start and end apart: 7, of which 6 were waited for; matrix products, arithmetic and copies ran while one was open for 11% of the time, Pallas kernels for 0%

commit v1 on v0

--- a/solution.py
+++ b/solution.py
@@ -108,7 +108,7 @@
         scatter_dimension=0,
         tiled=True,
     )
-    total = lax.psum(summed, "dp").astype(jnp.float32)
+    total = jnp.sum(lax.all_gather(summed, "dp"), axis=0).astype(jnp.float32)
     attended = attended_heads.reshape(rows_here, width)
     return (attended[None], grad_input[None], total.astype(jnp.bfloat16))
 

time: 665 us -> 619 us (0.931)
  waiting for transfers between devices: 482 us -> 436 us
    psum x1 -> x0, waiting for transfers between devices: 130 us -> none  [on_device(): total = lax.psum(summed, 'dp').astype(jnp.float32)]
    reduce_scatter x0 -> x1, waiting for transfers between devices: none -> 102 us  [on_device(): lax.psum_scatter(lax.optimization_barrier(term.astype(jnp.bfloat16)).asty...]
    unnamed x8 -> x7, waiting for transfers between devices: 102 us -> 2.48 us
    all_gather x0 -> x1, waiting for transfers between devices: none -> 81.2 us  [on_device(): total = jnp.sum(lax.all_gather(summed, 'dp'), axis=0).astype(jnp.float32)]
    unnamed x20 -> x18, local copies, waits for them, and re-layouts: 16.1 us -> 11.1 us
where the time goes in v1:
time: 619 us; the launch traced here: 617 us
  waiting for transfers between devices  436 us (70%)
  matrix products  73.6 us (12%)
  blocking collectives  40.9 us (7%)
  local copies, waits for them, and re-layouts  39.6 us (6%)
  between operations  14.3 us (2%)
  other arithmetic  12.3 us (2%)
    reduce_scatter x1, waiting for transfers between devices, on_device(): lax.psum_scatter(lax.optimization_barrier(term.astype(jnp.bfloat16)).asty...  102 us
    all_gather x1, waiting for transfers between devices, on_device(): total = jnp.sum(lax.all_gather(summed, 'dp'), axis=0).astype(jnp.float32)  81.2 us
    all_gather x1, waiting for transfers between devices, on_device(): weights = lax.all_gather(w_qkv, 'seq', axis=0, tiled=True)  76.5 us
    all_gather x1, waiting for transfers between devices, on_device(): lax.all_gather(values_here, 'seq', axis=0, tiled=True)  58.5 us
    all_gather x1, waiting for transfers between devices, on_device(): lax.all_gather(keys_here, 'seq', axis=0, tiled=True)  58.3 us
    all_gather x1, waiting for transfers between devices, on_device(): lax.all_gather(grad_out, 'seq', axis=0, tiled=True)  57.5 us
    all_gather x1, blocking collectives, on_device(): lax.all_gather(log_total.T, 'seq', axis=0, tiled=True)  20.5 us
    all_gather x1, blocking collectives, on_device(): lax.all_gather(delta_rows, 'seq', axis=0, tiled=True)  20.3 us
  transfers between devices with their start and end apart: 7, of which 6 were waited for; matrix products, arithmetic and copies ran while one was open for 11% of the time, Pallas kernels for 0%

profile of v1, /device:TPU:2, one launch (start us, length us, event | category | flops | bytes accessed | tf_op | source)
XLA Modules:
  0.0 617.1 jit_solution(13768137149208812614)
XLA Ops:
  7.2 0.7 all-gather.11.cloned.1.call-update
  8.0 0.7 all-gather.19.cloned.1.call-update
  8.7 76.5 %all-gather.11.cloned.1.call-done = bf16[1536,2304]{1,0:T(8,128)(2,1)} async-done(((bf16[96,2304]{1,0:T(8,128)(2,1)}), bf16[1536,2304]{1,0:T(8,128)(2,1)}) %all-gather.11.cloned.1.call-update) | async-done | bytes 7077904 | tf_op jit(solution)/shard_map/all_gather | solution.py:19
  85.2 4.5 convolution_convert_fusion.1
  89.7 1.0 slice_bitcast_fusion.2
  90.8 0.5 all-gather.15.cloned.1.call-update
  91.4 0.5 all-gather.17.cloned.1.call-update
  92.0 0.3 reshape_squeeze.3
  92.3 57.5 %all-gather.19.cloned.1.call-done = bf16[1,3072,768]{2,1,0:T(8,128)(2,1)} async-done(((bf16[1,192,768]{2,1,0:T(8,128)(2,1)}), bf16[1,3072,768]{2,1,0:T(8,128)(2,1)}) %all-gather.19.cloned.1.call-update) | async-done | bytes 4718608 | tf_op jit(solution)/shard_map/all_gather | solution.py:65
  149.8 6.7 %copy.46 = bf16[1,3072,768]{1,2,0:T(8,128)(2,1)} copy(bf16[1,3072,768]{2,1,0:T(8,128)(2,1)} %all-gather.19.cloned.1.call-done) | data formatting | bytes 9437184 | tf_op jit(solution)/shard_map/all_gather | solution.py:65
  156.5 58.5 %all-gather.13.cloned.1.call-done = bf16[3072,768]{1,0:T(8,128)(2,1)} async-done(((bf16[192,768]{1,0:T(8,128)(2,1)}), bf16[3072,768]{1,0:T(8,128)(2,1)}) %all-gather.13.cloned.1.call-update) | async-done | bytes 4718608 | tf_op jit(solution)/shard_map/all_gather | solution.py:29
  215.0 6.7 %copy.31 = bf16[3072,768]{0,1:T(8,128)(2,1)} copy(bf16[3072,768]{1,0:T(8,128)(2,1)} %all-gather.13.cloned.1.call-done) | data formatting | bytes 9437184 | tf_op jit(solution)/shard_map/all_gather | solution.py:29
  221.7 58.3 %all-gather.15.cloned.1.call-done = bf16[3072,768]{1,0:T(8,128)(2,1)} async-done(((bf16[192,768]{1,0:T(8,128)(2,1)}), bf16[3072,768]{1,0:T(8,128)(2,1)}) %all-gather.15.cloned.1.call-update) | async-done | bytes 4718608 | tf_op jit(solution)/shard_map/all_gather | solution.py:28
  280.0 6.7 %copy.32 = bf16[3072,768]{0,1:T(8,128)(2,1)} copy(bf16[3072,768]{1,0:T(8,128)(2,1)} %all-gather.15.cloned.1.call-done) | data formatting | bytes 9437184 | tf_op jit(solution)/shard_map/all_gather | solution.py:28
  286.7 9.6 %multiply_reduce_fusion = (f32[6,192]{1,0:T(8,128)S(1)}, f32[6,192,3072]{2,1,0:T(8,128)}) fusion(bf16[3072,6,128]{0,2,1:T(8,128)(2,1)} %bitcast.95, bf16[24,6,8,128]{3,2,1,0:T(8,128)(2,1)S(1)} %get-tuple-element.4), kind=kOutput, calls=%fused_computation.11 | convolution fusion | flops 913046400 | bytes 19173888 | tf_op jit(solution)/shard_map/qhd,khd->hqk/dot_general | solution.py:35
  296.3 7.5 %exponential_reduce_fusion = f32[6,192]{1,0:T(8,128)S(1)} fusion(f32[6,192,3072]{2,1,0:T(8,128)} %get-tuple-element.10, f32[6,192]{1,0:T(8,128)S(1)} %get-tuple-element.9), kind=kLoop, calls=%fused_computation.8 | loop fusion | flops 10615680 | bytes 14164992 | tf_op jit(solution)/shard_map/reduce_sum | solution.py:39
  303.8 8.5 %multiply_reduce_fusion.1 = (f32[192,6]{0,1:T(8,128)S(1)}, bf16[192,6,128]{2,0,1:T(8,128)(2,1)}) fusion(bf16[192,6,128]{2,1,0:T(8,128)(2,1)S(1)} %reshape_squeeze.3, bf16[3072,6,128]{0,2,1:T(8,128)(2,1)S(1)} %bitcast.105, f32[6,192,3072]{2,1,0:T(8,128)} %get-tuple-element.10, f32[6,192]{1,0:T(8,128)S(1)} %log_add_fusion), kind=kOutput, calls=%fused_computation.37 | convolution fusion | flops 917322624 | bytes 19473408 | tf_op jit(solution)/shard_map/hqk,khd->qhd/dot_general | solution.py:42
  312.3 20.3 %all-gather.3 = f32[16,192,6]{1,2,0:T(8,128)S(1)} all-gather(f32[1,192,6]{1,2,0:T(8,128)S(1)} %bitcast.110), channel_id=1, replica_groups=mesh['dp'=16,'seq'=16] {'seq'}, dimensions={0}, use_global_device_ids=true | all-gather | bytes 78336 | tf_op jit(solution)/shard_map/all_gather | solution.py:60
  332.8 20.5 %all-gather.2 = f32[16,192,6]{1,2,0:T(8,128)S(1)} all-gather(f32[1,192,6]{1,2,0:T(8,128)S(1)} %bitcast.109), channel_id=1, replica_groups=mesh['dp'=16,'seq'=16] {'seq'}, dimensions={0}, use_global_device_ids=true | all-gather | bytes 78336 | tf_op jit(solution)/shard_map/all_gather | solution.py:59
  353.5 10.7 %fusion.42 = bf16[6,24,8,128]{3,2,1,0:T(8,128)(2,1)S(1)} fusion(bf16[3072,6,128]{0,2,1:T(8,128)(2,1)} %bitcast.96, f32[6,192,3072]{2,1,0:T(8,128)} %get-tuple-element.10, f32[6,192]{1,0:T(8,128)S(1)} %bitcast.111, f32[6,192]{1,0:T(8,128)S(1)} %log_add_fusion, bf16[3072,6,128]{0,2,1:T(8,128)(2,1)} %bitcast.102, bf16[192,6,128]{2,1,0:T(8,128)(2,1)S(1)} %reshape_squeeze.3), kind=kOutput, calls=%fused_computation.33 | convolution fusion | flops 1833320448 | bytes 24192000 | tf_op jit(solution)/shard_map/hqk,khd->qhd/dot_general | solution.py:55
  364.3 6.7 %copy.42 = bf16[3072,768]{0,1:T(8,128)(2,1)} copy(bf16[3072,768]{1,0:T(8,128)(2,1)} %all-gather.17.cloned.1.call-done) | data formatting | bytes 9437184 | tf_op jit(solution)/shard_map/all_gather | solution.py:64
  371.0 9.4 %fusion.54 = f32[6,3072,192]{1,2,0:T(8,128)} fusion(bf16[3072,6,128]{0,2,1:T(8,128)(2,1)} %bitcast.97, bf16[24,6,8,128]{3,2,1,0:T(8,128)(2,1)S(1)} %get-tuple-element.5), kind=kOutput, calls=%fused_computation.43 | convolution fusion | flops 905969664 | bytes 19169280 | tf_op jit(solution)/shard_map/qhd,khd->hqk/dot_general | solution.py:69
  380.3 8.8 %fusion.36 = bf16[6,24,8,128]{3,2,1,0:T(8,128)(2,1)S(1)} fusion(bf16[3072,6,128]{0,2,1:T(8,128)(2,1)} %bitcast.100, f32[6,3072,192]{1,2,0:T(8,128)} %fusion.54, f32[6,3072]{1,0:T(8,128)S(1)} %bitcast.107), kind=kOutput, calls=%fused_computation.31 | convolution fusion | flops 916733952 | bytes 19243008 | tf_op jit(solution)/shard_map/hqk,qhd->khd/dot_general | solution.py:73
  389.1 10.9 %fusion.45 = bf16[6,24,8,128]{3,2,1,0:T(8,128)(2,1)S(1)} fusion(bf16[3072,6,128]{0,2,1:T(8,128)(2,1)} %bitcast.98, f32[6,3072,192]{1,2,0:T(8,128)} %fusion.54, f32[6,3072]{1,0:T(8,128)S(1)} %bitcast.106, f32[6,3072]{1,0:T(8,128)} %bitcast.108, bf16[3072,6,128]{0,2,1:T(8,128)(2,1)} %bitcast.101, bf16[24,6,8,128]{3,2,1,0:T(8,128)(2,1)S(1)} %get-tuple-element.3), kind=kOutput, calls=%fused_computation.34 | convolution fusion | flops 1833320448 | bytes 24330240 | tf_op jit(solution)/shard_map/hqk,qhd->khd/dot_general | solution.py:85
  400.1 5.0 fusion.6
  405.1 9.8 %copy.63 = bf16[1536,2304]{1,0:T(8,128)(2,1)} copy(bf16[1536,2304]{0,1:T(8,128)(2,1)} %fusion.6) | data formatting | bytes 14155776
  415.0 101.7 %reduce-scatter.4.cloned.1.call-done = bf16[96,2304]{1,0:T(8,128)(2,1)} async-done(((bf16[1536,2304]{1,0:T(8,128)(2,1)}), bf16[96,2304]{1,0:T(8,128)(2,1)}) %reduce-scatter.4.cloned.1.call-update) | async-done | bytes 442384 | tf_op jit(solution)/shard_map/reduce_scatter | solution.py:103
  516.7 0.2 copy.36
  516.9 1.1 broadcast_in_dim_reshape.3
  518.0 6.3 %fusion.23 = bf16[1,192,1536]{2,1,0:T(8,128)(2,1)} fusion(bf16[192,2304]{1,0:T(8,128)(2,1)S(1)} %bitcast_dynamic-update-slice_fusion, bf16[1536,2304]{1,0:T(8,128)(2,1)} %all-gather.11.cloned.1.call-done), kind=kOutput, calls=%fused_computation.26 | convolution fusion | flops 1359249408 | bytes 8552448 | tf_op jit(solution)/shard_map/dot_general | solution.py:97
  524.2 81.2 %all-gather.21.cloned.1.call-done = bf16[1536,2304]{1,0:T(8,128)(2,1)} async-done(((bf16[96,2304]{1,0:T(8,128)(2,1)}), bf16[1536,2304]{1,0:T(8,128)(2,1)}) %all-gather.21.cloned.1.call-update) | async-done | bytes 7077904 | tf_op jit(solution)/shard_map/all_gather | solution.py:111
  605.4 4.9 reduce_sum.32
  (32 shorter events, 0.8 us)
Async XLA Ops:
  7.2 78.0 %copy-start = (bf16[1,192,1536]{2,1,0:T(8,128)(2,1)S(1)}, bf16[1,192,1536]{2,1,0:T(8,128)(2,1)}, u32[]{:S(2)}) copy-start(bf16[1,192,1536]{2,1,0:T(8,128)(2,1)} %param.3) | copy-start | bytes 1769476
  7.2 78.0 %all-gather.11.cloned.1.call-start = ((), (), s32[]{:S(2)}) async-start(), calls=%async_computation.1 | async-start | bytes 7520256 | tf_op jit(solution)/shard_map/all_gather | solution.py:19
  7.9 141.9 %all-gather.19.cloned.1.call-start = ((), (), s32[]{:S(2)}) async-start(), calls=%async_computation.5 | async-start | bytes 5013504 | tf_op jit(solution)/shard_map/all_gather | solution.py:65
  8.7 83.3 %copy-start.1 = (bf16[1,192,768]{2,1,0:T(8,128)(2,1)S(1)}, bf16[1,192,768]{2,1,0:T(8,128)(2,1)}, u32[]{:S(2)}) copy-start(bf16[1,192,768]{2,1,0:T(8,128)(2,1)} %param.5) | copy-start | bytes 884740
  8.7 206.3 %all-gather.13.cloned.1.call-start = ((), (), s32[]{:S(2)}) async-start(), calls=%async_computation.2 | async-start | bytes 5013504 | tf_op jit(solution)/shard_map/all_gather | solution.py:29
  90.8 189.2 %all-gather.15.cloned.1.call-start = ((), (), s32[]{:S(2)}) async-start(), calls=%async_computation.3 | async-start | bytes 5013504 | tf_op jit(solution)/shard_map/all_gather | solution.py:28
  91.3 272.9 %all-gather.17.cloned.1.call-start = ((), (), s32[]{:S(2)}) async-start(), calls=%async_computation.4 | async-start | bytes 5013504 | tf_op jit(solution)/shard_map/all_gather | solution.py:64
  91.9 424.7 %reduce-scatter.4.cloned.1.call-start = ((), (), s32[]{:S(2)}) async-start(), calls=%async_computation.7 | async-start | bytes 7520256 | tf_op jit(solution)/shard_map/reduce_scatter | solution.py:103
  280.0 23.8 %slice-start = ((s8[4718592]{0:T(1024)(128)(4,1)}), s8[524288]{0:T(1024)(128)(4,1)S(1)}, s32[]{:S(2)}) async-start(s8[4718592]{0:T(1024)(128)(4,1)} %bitcast.103), calls=%async_computation.8 | async-start | bytes 1048576
  286.7 17.1 %slice-start.1 = ((s8[4718592]{0:T(1024)(128)(4,1)}), s8[4194304]{0:T(1024)(128)(4,1)S(1)}, s32[]{:S(2)}) async-start(s8[4718592]{0:T(1024)(128)(4,1)} %bitcast.103), calls=%async_computation.9 | async-start | bytes 8388608
  353.5 26.9 %copy-start.3 = (f32[3072,6]{0,1:T(8,128)}, f32[3072,6]{0,1:T(8,128)S(1)}, u32[]{:S(2)}) copy-start(f32[3072,6]{0,1:T(8,128)S(1)} %reshape.60) | copy-start | bytes 221188
  414.9 101.8 %copy-start.2 = (bf16[192,6,128]{2,0,1:T(8,128)(2,1)S(1)}, bf16[192,6,128]{2,0,1:T(8,128)(2,1)}, u32[]{:S(2)}) copy-start(bf16[192,6,128]{2,0,1:T(8,128)(2,1)} %get-tuple-element.12) | copy-start | bytes 884740
  414.9 190.5 %all-gather.21.cloned.1.call-start = ((), (), s32[]{:S(2)}) async-start(), calls=%async_computation.6 | async-start | bytes 7520256 | tf_op jit(solution)/shard_map/all_gather | solution.py:111
Sparse Core Ops, SparseCore 0:
  10.7 74.4 all-gather.10
  87.9 61.8 all-gather.18
  153.1 61.8 all-gather.12
  218.1 61.8 all-gather.14
  283.1 62.3 all-gather.16
  415.0 101.5 reduce-scatter.3
  518.4 86.9 all-gather.20
